TPU v7x, 32 devices: a whole 2x2x4 slice. The times are simulated.
32 devices in a mesh: band: 4 (over y, x), patch: 8 (over z, core).
Axes of the slice: x: 2, y: 2, z: 4, core: 2. Of those that a mesh axis runs over, the one named last changes fastest.
Arguments:
- images: float32 [4, 256, 168, 168], P('band', 'patch'), may hold values from -48 to 48
- coeffs: bfloat16 [4, 256, 3, 128, 128], P('band', 'patch'), may hold values from 0.29882812 to 1.5
- inverse_var: float32 [4, 256, 128, 128], P('band', 'patch'), may hold values from 0.3 to 3
- bad_lines: int32 [4, 256, 2], P('band', 'patch'), may hold values from 0 to 127
- destinations: int32 [4, 256, 1], P('band', 'patch'), may hold values from 0 to 7; in each aligned block of 32 rows (0 to 31, 32 to 63, ..., all dimensions but the last counted through in order) at most 8 rows name the same one
- tile_slots: int32 [4, 256], P('band', 'patch'), may hold values from 0 to 15
Outputs:
- coadd: float32 [4, 8, 256, 1024], P('band', 'patch')
- detection: float32 [8, 256, 1024], P('patch', 'band')
Inputs may be any that keep to these rules, and one draw needn't show every extreme that they name: `destinations`: among the 32 pieces of one band held by one index of patch (aligned blocks), no patch is named more than 8 times, a bound that some block reaches.
All inputs are finite; a program needn't handle non-finite values.
Results may differ from a plain program's by a relative error of at most 0.00035.
Values sent between devices are 32-bit elements; how exact they have to be, the bound alone decides.
A program may use at most 192 MiB of HBM per device.

v0:
```python
import jax
import jax.numpy as jnp
from jax import lax
from jax.sharding import PartitionSpec as P

TILES_X = 8
TILES_Y = 2


HIGHEST = lax.Precision.HIGHEST
FRACTIONS = (0.12, 0.25, 0.45)
FLOOR = 0.5


def kernel_bands(tile_side, half_taps):
    offset = (
        jnp.arange(tile_side + 2 * half_taps, dtype=jnp.int32)[None, :]
        - jnp.arange(tile_side, dtype=jnp.int32)[:, None]
    )
    inside = (offset >= 0) & (offset <= 2 * half_taps)
    centred = (offset - half_taps).astype(jnp.float32)
    tap_offsets = (jnp.arange(2 * half_taps + 1, dtype=jnp.int32) - half_taps).astype(jnp.float32)
    matrices = []
    for fraction in FRACTIONS:
        sigma_width = fraction * half_taps
        tap_total = jnp.sum(jnp.exp(-0.5 * (tap_offsets / sigma_width) ** 2))
        matrices.append(
            jnp.where(inside, jnp.exp(-0.5 * (centred / sigma_width) ** 2) / tap_total, 0.0)
        )
    return jnp.stack(matrices)


def match_pieces(images, coeffs, bands):
    rows_done = jnp.einsum("kyi,pij->pkyj", bands, images, precision=HIGHEST)
    smoothed = jnp.einsum("pkyj,kxj->pkyx", rows_done, bands, precision=HIGHEST)
    return jnp.sum(coeffs * smoothed, axis=1)


def slot_matrix(targets, tile_index, owners_count, slot_depth):
    owners = jnp.arange(owners_count, dtype=jnp.int32)
    onehot = (targets[:, None] == owners[None, :]).astype(jnp.int32)
    before = jnp.cumsum(onehot, axis=0) - onehot
    slot_rank = jnp.sum(before * onehot, axis=1)
    slot_index = targets * slot_depth + slot_rank
    slot_range = jnp.arange(owners_count * slot_depth, dtype=jnp.int32)
    chosen = slot_range[:, None] == slot_index[None, :]
    selector = chosen.astype(jnp.float32)
    position = jnp.sum(jnp.where(chosen, tile_index[None, :] + 1, 0), axis=1) - 1
    return (selector, position.astype(jnp.float32).reshape(owners_count, slot_depth))


def pack_slots(selector, slot_data, owners_count, slot_depth):
    flat_rows = slot_data.reshape(slot_data.shape[0], -1)
    packed = jnp.dot(selector, flat_rows, precision=HIGHEST, preferred_element_type=jnp.float32)
    return packed.reshape((owners_count, slot_depth) + slot_data.shape[1:])


def per_device(images, coeffs, inverse_var, bad_lines, destinations, tile_slots):
    owners_count = lax.axis_size("patch")
    piece_count = images.shape[1]
    slot_depth = max(2, 2 * piece_count // owners_count)
    tile_side = inverse_var.shape[-1]
    half_taps = (images.shape[-1] - tile_side) // 2
    bands = kernel_bands(tile_side, half_taps)
    line_index = jnp.arange(tile_side, dtype=jnp.int32)
    lines = bad_lines[0]
    keep_pixel = (line_index[None, :, None] != lines[:, 0][:, None, None]) & (
        line_index[None, None, :] != lines[:, 1][:, None, None]
    )
    weight = jnp.where(keep_pixel, inverse_var[0], 0.0)
    selector, position = slot_matrix(destinations[0, :, 0], tile_slots[0], owners_count, slot_depth)
    raw_slots = pack_slots(selector, images[0], owners_count, slot_depth)
    coeff_slots = pack_slots(selector, coeffs[0].astype(jnp.float32), owners_count, slot_depth)
    weight_slots = pack_slots(selector, weight, owners_count, slot_depth)
    image_part = lax.all_to_all(raw_slots, "patch", split_axis=0, concat_axis=0, tiled=True)
    coeff_part = lax.all_to_all(coeff_slots, "patch", split_axis=0, concat_axis=0, tiled=True)
    weight_part = lax.all_to_all(weight_slots, "patch", split_axis=0, concat_axis=0, tiled=True)
    place_part = lax.all_to_all(position, "patch", split_axis=0, concat_axis=0, tiled=True)
    lead_shape = image_part.shape[:2]
    matched = match_pieces(
        image_part.reshape((-1,) + image_part.shape[2:]),
        coeff_part.reshape((-1,) + coeff_part.shape[2:]),
        bands,
    )
    matched = matched.reshape(lead_shape + (tile_side, tile_side))
    numer_slots = weight_part * matched
    flat_places = place_part.reshape(-1)
    tile_targets = jnp.arange(TILES_Y * TILES_X, dtype=jnp.float32)
    spread = (tile_targets[:, None] == flat_places[None, :]).astype(jnp.float32)

    def assemble(planes):
        summed = jnp.dot(
            spread,
            planes.reshape(flat_places.shape[0], -1),
            precision=HIGHEST,
            preferred_element_type=jnp.float32,
        )
        return (
            summed.reshape(TILES_Y, TILES_X, tile_side, tile_side)
            .transpose(0, 2, 1, 3)
            .reshape(TILES_Y * tile_side, TILES_X * tile_side)
        )

    numerator = assemble(numer_slots)
    denominator = assemble(weight_part)
    coadd = numerator / jnp.maximum(denominator, FLOOR)
    detection = lax.psum_scatter(numerator * coadd, "band", scatter_dimension=0, tiled=True)
    return (coadd[None, None], detection[None])


def solution(mesh):
    in_specs = (
        P("band", "patch", None, None),
        P("band", "patch", None, None, None),
        P("band", "patch", None, None),
        P("band", "patch", None),
        P("band", "patch", None),
        P("band", "patch"),
    )
    out_specs = (P("band", "patch", None, None), P("patch", "band", None))
    return jax.shard_map(
        per_device, mesh=mesh, in_specs=in_specs, out_specs=out_specs, check_vma=False
    )
```

profile of v0, /device:TPU:0, one launch (start us, length us, event | category | flops | bytes accessed | tf_op | source)
XLA Modules:
  0.0 722.4 jit_solution(11556979796788347800)
XLA Ops:
  7.2 0.7 fusion.30
  7.9 0.1 reduce_window_sum.11
  7.9 0.8 select_reduce_fusion.1
  8.8 0.7 multiply_add_fusion.2
  9.4 0.7 add_bitcast_fusion
  10.1 0.1 select_reduce_fusion
  10.2 0.7 convert_element_type.51
  10.9 6.3 all-to-all-start
  17.2 6.0 reshape_squeeze.3
  23.2 7.0 dot_general.48
  30.2 14.0 %fusion.3 = f32[8,8,168,168]{3,1,2,0:T(8,128)} fusion(f32[168,168,32]{1,0,2:T(8,128)} %dot_general.48, s32[32]{0:T(128)S(1)} %multiply_add_fusion.2, s32[8,8]{1,0:T(8,128)S(1)} %multiply_add_fusion), kind=kOutput, calls=%fused_computation.4 | convolution fusion | flops 693635072 | bytes 10838400 | tf_op jit(solution)/shard_map/dot_general | solution.py:54
  44.2 0.0 all-to-all-done
  44.2 5.3 all-to-all-start.3
  49.4 3.4 reshape.316
  52.8 0.7 copy.54
  53.5 6.8 fusion.12
  60.3 0.0 copy-start.1
  60.3 0.0 copy-start
  60.3 229.2 %all-to-all-done.3 = f32[8,8,168,168]{3,1,2,0:T(8,128)} async-done(((f32[8,8,168,168]{3,1,2,0:T(8,128)}), f32[8,8,168,168]{3,1,2,0:T(8,128)}, u32[]{:S(2)}, u32[]{:S(2)}) %all-to-all-start.3) | async-done | bytes 7225376 | tf_op jit(solution)/shard_map/all_to_all | solution.py:75
  289.5 16.4 %all-to-all-start.2 = ((f32[8,8,3,128,128]{4,1,3,2,0:T(8,128)}), f32[8,8,3,128,128]{4,1,3,2,0:T(8,128)}, u32[]{:S(2)}, u32[]{:S(2)}) async-start(f32[8,8,3,128,128]{4,1,3,2,0:T(8,128)} %fusion.12), calls=%async_computation.2 | async-start | bytes 25165824 | tf_op jit(solution)/shard_map/all_to_all | solution.py:76
  306.0 0.0 copy-done.1
  306.0 0.1 iota_compare_fusion
  306.1 0.7 broadcast_and_fusion
  306.8 0.0 copy-done
  306.8 5.5 fusion.16
  312.3 267.2 %all-to-all-done.2 = f32[8,8,3,128,128]{4,1,3,2,0:T(8,128)} async-done(((f32[8,8,3,128,128]{4,1,3,2,0:T(8,128)}), f32[8,8,3,128,128]{4,1,3,2,0:T(8,128)}, u32[]{:S(2)}, u32[]{:S(2)}) %all-to-all-start.2) | async-done | bytes 12582944 | tf_op jit(solution)/shard_map/all_to_all | solution.py:76
  579.5 4.6 all-to-all-start.1
  584.1 0.0 reduce-scatter.2.cloned.1.call-start
  584.1 0.6 exponential_reduce_fusion
  584.7 0.6 exponential_reduce_fusion.1
  585.4 0.6 exponential_reduce_fusion.2
  586.0 0.6 divide_select_fusion.2
  586.6 1.4 divide_select_fusion
  588.0 0.5 broadcast.317
  588.5 0.7 reduce.3
  589.1 0.1 eq.85
  589.2 7.4 %copy.34 = f32[8,8,168,168]{3,2,1,0:T(8,128)S(1)} copy(f32[8,8,168,168]{3,1,2,0:T(8,128)} %all-to-all-done.3) | data formatting | bytes 14450688 | tf_op jit(solution)/shard_map/all_to_all | solution.py:75
  596.6 25.2 %fusion.19 = f32[64,168,3,128]{3,1,0,2:T(8,128)} fusion(f32[64,168,168,1]{2,1,0,3:T(8,128)S(1)} %bitcast.143, f32[1,128,168]{1,2,0:T(8,128)S(1)} %get-tuple-element.8, f32[1,128,168]{1,2,0:T(8,128)S(1)} %get-tuple-element.9, f32[1,128,168]{1,2,0:T(8,128)S(1)} %divide_select_fusion.2), kind=kOutput, calls=%fused_computation.27 | convolution fusion | flops 8323725312 | bytes 23998464 | tf_op jit(solution)/shard_map/kyi,pij->pkyj/dot_general | solution.py:34
  621.8 11.2 %copy.32 = f32[8,8,3,128,128]{4,3,2,1,0:T(8,128)} copy(f32[8,8,3,128,128]{4,1,3,2,0:T(8,128)} %all-to-all-done.2) | data formatting | bytes 25165824 | tf_op jit(solution)/shard_map/all_to_all | solution.py:76
  633.0 12.6 %copy.36 = f32[64,3,128,128]{2,3,0,1:T(8,128)} copy(f32[64,3,128,128]{3,2,1,0:T(8,128)} %bitcast.144) | data formatting | bytes 25165824 | tf_op jit(solution)/shard_map/reshape | solution.py:82
  645.6 22.9 %fusion.2 = f32[64,128,128]{1,2,0:T(8,128)} fusion(f32[64,3,128,128]{2,3,0,1:T(8,128)} %copy.36, f32[64,168,3,128]{3,1,0,2:T(8,128)} %fusion.19, f32[1,128,168]{1,2,0:T(8,128)S(1)} %get-tuple-element.8, f32[1,128,168]{1,2,0:T(8,128)S(1)} %get-tuple-element.9, f32[1,128,168]{1,2,0:T(8,128)S(1)} %divide_select_fusion.2), kind=kOutput, calls=%fused_computation.3 | convolution fusion | flops 6347159552 | bytes 33550336 | tf_op jit(solution)/shard_map/pkyj,kxj->pkyx/dot_general | solution.py:35
  668.6 5.6 copy.38
  674.1 3.9 all-to-all-done.1
  678.1 5.1 fusion.10
  683.2 3.7 bitcast_divide_fusion
  686.9 1.4 divide_multiply_fusion
  688.4 0.0 reduce-scatter.2.cloned.1.call-update
  688.4 1.1 div.109
  689.5 25.6 %reduce-scatter.2.cloned.1.call-done = f32[64,1024]{1,0:T(8,128)} async-done(((f32[256,1024]{1,0:T(8,128)}), f32[64,1024]{1,0:T(8,128)}) %reduce-scatter.2.cloned.1.call-update) | async-done | bytes 262160 | tf_op jit(solution)/shard_map/reduce_scatter | solution.py:107
  (4 shorter events, 0.0 us)
Async XLA Ops:
  10.9 33.3 %all-to-all-start = ((f32[8,1,8]{2,1,0:T(1,128)}), f32[8,1,8]{2,1,0:T(1,128)S(1)}, u32[]{:S(2)}, u32[]{:S(2)}) async-start(f32[8,1,8]{2,1,0:T(1,128)} %bitcast.2), calls=%async_computation | async-start | bytes 8192 | tf_op jit(solution)/shard_map/all_to_all | solution.py:78
  44.2 245.3 %all-to-all-start.3 = ((f32[8,8,168,168]{3,1,2,0:T(8,128)}), f32[8,8,168,168]{3,1,2,0:T(8,128)}, u32[]{:S(2)}, u32[]{:S(2)}) async-start(f32[8,8,168,168]{3,1,2,0:T(8,128)} %fusion.3), calls=%async_computation.3 | async-start | bytes 22020096 | tf_op jit(solution)/shard_map/all_to_all | solution.py:75
  60.3 245.6 %copy-start.1 = (s32[1,32,2]{1,2,0:T(2,128)S(1)}, s32[1,32,2]{1,2,0:T(2,128)}, u32[]{:S(2)}) copy-start(s32[1,32,2]{1,2,0:T(2,128)} %param.9) | copy-start | bytes 772
  60.3 246.4 %copy-start = (f32[1,32,128,128]{3,2,1,0:T(8,128)S(1)}, f32[1,32,128,128]{3,2,1,0:T(8,128)}, u32[]{:S(2)}) copy-start(f32[1,32,128,128]{3,2,1,0:T(8,128)} %param.8) | copy-start | bytes 6291460
  289.5 290.0 %all-to-all-start.2 = ((f32[8,8,3,128,128]{4,1,3,2,0:T(8,128)}), f32[8,8,3,128,128]{4,1,3,2,0:T(8,128)}, u32[]{:S(2)}, u32[]{:S(2)}) async-start(f32[8,8,3,128,128]{4,1,3,2,0:T(8,128)} %fusion.12), calls=%async_computation.2 | async-start | bytes 25165824 | tf_op jit(solution)/shard_map/all_to_all | solution.py:76
  579.5 98.6 %all-to-all-start.1 = ((f32[8,8,128,128]{3,1,2,0:T(8,128)}), f32[8,8,128,128]{3,1,2,0:T(8,128)}, u32[]{:S(2)}, u32[]{:S(2)}) async-start(f32[8,8,128,128]{3,1,2,0:T(8,128)} %fusion.16), calls=%async_computation.1 | async-start | bytes 8388608 | tf_op jit(solution)/shard_map/all_to_all | solution.py:77
  584.1 131.1 %reduce-scatter.2.cloned.1.call-start = ((), (), s32[]{:S(2)}) async-start(), calls=%async_computation.5 | async-start | bytes 1310720 | tf_op jit(solution)/shard_map/reduce_scatter | solution.py:107
Sparse Core Ops, SparseCore 0:
  688.5 26.5 reduce-scatter.1
where the time goes:
time: 725 us; the launch traced here: 722 us
  waiting for transfers between devices  526 us (73%)
  matrix products  83.3 us (11%)
  local copies, waits for them, and re-layouts  56.2 us (8%)
  starting transfers between devices  32.6 us (4%)
  between operations  14.6 us (2%)
  other arithmetic  9.76 us (1%)
    all_to_all x1, waiting for transfers between devices, per_device(): lax.all_to_all(coeff_slots, 'patch', split_axis=0, concat_axis=0, tiled=T...  267 us
    all_to_all x1, waiting for transfers between devices, per_device(): lax.all_to_all(raw_slots, 'patch', split_axis=0, concat_axis=0, tiled=True)  229 us
    dot_general x3, matrix products, pack_slots(): jnp.dot(selector, flat_rows, precision=HIGHEST, preferred_element_type=jn...  26.4 us
    reduce_scatter x1, waiting for transfers between devices, per_device(): lax.psum_scatter(numerator * coadd, 'band', scatter_dimension=0, tiled=True)  25.6 us
    dot_general x1, matrix products, match_pieces(): rows_done = jnp.einsum('kyi,pij->pkyj', bands, images, precision=HIGHEST)  25.2 us
    dot_general x1, matrix products, match_pieces(): smoothed = jnp.einsum('pkyj,kxj->pkyx', rows_done, bands, precision=HIGHEST)  22.9 us
    all_to_all x1, starting transfers between devices, per_device(): lax.all_to_all(coeff_slots, 'patch', split_axis=0, concat_axis=0, tiled=T...  16.4 us
  transfers between devices with their start and end apart: 5, of which 4 were waited for; matrix products, arithmetic and copies ran while one was open for 19% of the time, Pallas kernels for 0%

commit v1 on v0

--- a/solution.py
+++ b/solution.py
@@ -1,6 +1,8 @@
 import jax
 import jax.numpy as jnp
 from jax import lax
+from jax.experimental import pallas as pl
+from jax.experimental.pallas import tpu as pltpu
 from jax.sharding import PartitionSpec as P
 
 TILES_X = 8
@@ -55,7 +57,7 @@
     return packed.reshape((owners_count, slot_depth) + slot_data.shape[1:])
 
 
-def per_device(images, coeffs, inverse_var, bad_lines, destinations, tile_slots):
+def exchanged_raw(images, coeffs, inverse_var, bad_lines, destinations, tile_slots):
     owners_count = lax.axis_size("patch")
     piece_count = images.shape[1]
     slot_depth = max(2, 2 * piece_count // owners_count)
@@ -108,6 +110,330 @@
     return (coadd[None, None], detection[None])
 
 
+TILES = TILES_Y * TILES_X
+GROUP = 4
+CHUNKS = 8
+MESH = pl.DeviceIdType.MESH
+
+
+def split(value):
+    high = value.astype(jnp.bfloat16)
+    return high, (value - high.astype(jnp.float32)).astype(jnp.bfloat16)
+
+
+def dot(a, b):
+    return jnp.dot(a, b, preferred_element_type=jnp.float32)
+
+
+def match_kernel(lines_ref, image_ref, coeff_ref, var_ref, rows_ref, cols_ref, out_ref):
+    step = pl.program_id(0)
+    side = var_ref.shape[-1]
+    count = out_ref.shape[0] // (2 * side)
+    row = lax.broadcasted_iota(jnp.int32, (side, side), 0)
+    col = lax.broadcasted_iota(jnp.int32, (side, side), 1)
+    for i in range(GROUP):
+        piece = step * GROUP + i
+        high, low = split(image_ref[i])
+        done = dot(rows_ref[0], high) + dot(rows_ref[0], low) + dot(rows_ref[1], high)
+        high, low = split(done)
+        matched = None
+        for k in range(coeff_ref.shape[1]):
+            ys = slice(k * side, (k + 1) * side)
+            both = dot(high[ys], cols_ref[k])
+            smooth = both[:, :side] + both[:, side:] + dot(low[ys], cols_ref[k, :, :side])
+            term = coeff_ref[i, k].astype(jnp.float32) * smooth
+            matched = term if matched is None else matched + term
+        masked = (row == lines_ref[piece, 0]) | (col == lines_ref[piece, 1])
+        weight = jnp.where(masked, 0.0, var_ref[i])
+        out_ref[pl.ds(piece, side, stride=2 * count), :] = weight * matched
+        out_ref[pl.ds(count + piece, side, stride=2 * count), :] = weight
+
+
+def match_local(images, coeffs, inverse_var, lines, bands):
+    count, wide, _ = images.shape
+    kernels, side, _ = bands.shape
+    rounded = lax.reduce_precision(bands, 8, 7)
+    high, low = rounded.astype(jnp.bfloat16), (bands - rounded).astype(jnp.bfloat16)
+    rows = jnp.stack([high.reshape(kernels * side, wide), low.reshape(kernels * side, wide)])
+    cols = jnp.concatenate([jnp.swapaxes(high, 1, 2), jnp.swapaxes(low, 1, 2)], axis=2)
+    out = pl.pallas_call(
+        match_kernel,
+        out_shape=jax.ShapeDtypeStruct((side * 2 * count, side), jnp.float32),
+        grid_spec=pltpu.PrefetchScalarGridSpec(
+            num_scalar_prefetch=1,
+            grid=(count // GROUP,),
+            in_specs=[
+                pl.BlockSpec((GROUP, wide, wide), lambda i, _: (i, 0, 0)),
+                pl.BlockSpec((GROUP, kernels, side, side), lambda i, _: (i, 0, 0, 0)),
+                pl.BlockSpec((GROUP, side, side), lambda i, _: (i, 0, 0)),
+                pl.BlockSpec(rows.shape, lambda i, _: (0, 0, 0)),
+                pl.BlockSpec(cols.shape, lambda i, _: (0, 0, 0)),
+            ],
+            out_specs=pl.BlockSpec((side * 2 * count, side), lambda i, _: (0, 0)),
+        ),
+        compiler_params=pltpu.CompilerParams(vmem_limit_bytes=48 * 1024 * 1024),
+        cost_estimate=pl.CostEstimate(
+            flops=count * 36 * kernels * side * wide * side, bytes_accessed=14 << 20, transcendentals=0
+        ),
+    )(lines, images, coeffs, inverse_var, rows, cols)
+    return out.reshape(side, 2, count, side)
+
+
+def line_kernel(
+    data, pick, total,
+    units, listed, summed, to_across, to_outer, from_inner, own_sum, to_sib, from_sib,
+    local_sem, share_send, share_recv, list_send, list_recv, across_send, across_recv,
+    outer_send, outer_recv, final_send, final_recv,
+):
+    me = lax.axis_index("patch")
+    z, core = me // 2, me % 2
+    half_rows = units.shape[0]
+    step_rows = half_rows // CHUNKS
+    side = z // 2
+    is_outer = (z == 0) | (z == 3)
+    is_inner = (z == 1) | (z == 2)
+    sibling = {"patch": z * 2 + 1 - core}
+    inward = {"patch": (1 + side) * 2 + core}
+    outward = {"patch": 3 * side * 2 + core}
+    across = {"patch": (2 - side) * 2 + core}
+    pieces = data.shape[2]
+
+    barrier = pltpu.get_barrier_semaphore()
+    pl.semaphore_signal(barrier, inc=1, device_id=sibling, device_id_type=MESH)
+
+    @pl.when(is_outer)
+    def _():
+        pl.semaphore_signal(barrier, inc=1, device_id=inward, device_id_type=MESH)
+        pl.semaphore_wait(barrier, 2)
+
+    @pl.when(is_inner)
+    def _():
+        pl.semaphore_signal(barrier, inc=1, device_id=outward, device_id_type=MESH)
+        pl.semaphore_signal(barrier, inc=1, device_id=across, device_id_type=MESH)
+        pl.semaphore_wait(barrier, 3)
+
+    def rows_of(i):
+        return pl.ds(i * step_rows, step_rows)
+
+    def remote(source, target, send, recv, device):
+        return pltpu.make_async_remote_copy(
+            src_ref=source, dst_ref=target, send_sem=send, recv_sem=recv,
+            device_id=device, device_id_type=MESH,
+        )
+
+    def share(i):
+        return remote(
+            data.at[pl.ds((1 - core) * half_rows + i * step_rows, step_rows)],
+            units.at[rows_of(i), :, pl.ds(pieces, pieces)],
+            share_send.at[i], share_recv.at[i], sibling,
+        )
+
+    def send_list(i):
+        return remote(units.at[rows_of(i)], listed.at[rows_of(i)], list_send.at[i], list_recv.at[i], inward)
+
+    def send_across(i):
+        return remote(to_across.at[rows_of(i)], summed.at[rows_of(i)], across_send.at[i], across_recv.at[i], across)
+
+    def send_outer(i):
+        return remote(to_outer.at[rows_of(i)], from_inner.at[rows_of(i)], outer_send.at[i], outer_recv.at[i], outward)
+
+    def send_final(i):
+        return remote(to_sib.at[rows_of(i)], from_sib.at[rows_of(i)], final_send.at[i], final_recv.at[i], sibling)
+
+    own_copy = pltpu.make_async_copy(
+        data.at[pl.ds(core * half_rows, half_rows)], units.at[:, :, pl.ds(0, pieces)], local_sem
+    )
+    own_copy.start()
+
+    @pl.loop(0, CHUNKS)
+    def _(i):
+        share(i).start()
+
+    own_copy.wait()
+
+    def placed(y, row_from, with_list):
+        parts = []
+        for q in range(2):
+            value = units[y, q]
+            if with_list:
+                value = jnp.concatenate([value, listed[y, q]], axis=0)
+            parts.append(value)
+        high, low = split(jnp.concatenate(parts, axis=1))
+        both = jnp.concatenate([high, low], axis=0)
+        wide = pick.shape[1] // 2
+        if with_list:
+            chosen = pick[pl.ds(row_from, pick.shape[0] - row_from), :]
+        else:
+            chosen = pick[pl.ds(row_from, pick.shape[0] - row_from), pl.ds(0, wide)]
+        return dot(chosen, both)
+
+    def finish(y, extra):
+        for q in range(2):
+            value = own_sum[y, q] + extra[y, q, -32:]
+            total[core * half_rows + y, q] = value[:TILES]
+            to_sib[y, q] = value[TILES:]
+
+    @pl.when(is_outer)
+    def _():
+        @pl.loop(0, CHUNKS + 2)
+        def _(i):
+            @pl.when(i < CHUNKS)
+            def _():
+                share(i).wait_recv()
+                send_list(i).start()
+
+                @pl.loop(0, step_rows)
+                def _(r):
+                    y = i * step_rows + r
+                    value = placed(y, 6 * TILES, False)
+                    lanes = value.shape[1] // 2
+                    for q in range(2):
+                        own_sum[y, q] = value[:, q * lanes:(q + 1) * lanes]
+
+            @pl.when(i >= 2)
+            def _():
+                j = i - 2
+                send_outer(j).wait_recv()
+
+                @pl.loop(0, step_rows)
+                def _(r):
+                    finish(j * step_rows + r, from_inner)
+
+                send_final(j).start()
+
+        @pl.loop(0, CHUNKS)
+        def _(i):
+            send_list(i).wait_send()
+
+    @pl.when(is_inner)
+    def _():
+        @pl.loop(0, CHUNKS + 2)
+        def _(i):
+            @pl.when(i < CHUNKS)
+            def _():
+                share(i).wait_recv()
+                send_list(i).wait_recv()
+
+                @pl.loop(0, step_rows)
+                def _(r):
+                    y = i * step_rows + r
+                    value = placed(y, 0, True)
+                    lanes = value.shape[1] // 2
+                    for q in range(2):
+                        here = value[:, q * lanes:(q + 1) * lanes]
+                        to_across[y, q] = here[:4 * TILES]
+                        to_outer[y, q] = here[4 * TILES:6 * TILES]
+                        own_sum[y, q] = here[6 * TILES:]
+
+                send_across(i).start()
+
+            @pl.when(i >= 2)
+            def _():
+                j = i - 2
+                send_across(j).wait_recv()
+
+                @pl.loop(0, step_rows)
+                def _(r):
+                    y = j * step_rows + r
+                    for q in range(2):
+                        to_outer[y, q] = to_outer[y, q] + summed[y, q, :2 * TILES]
+                    finish(y, summed)
+
+                send_outer(j).start()
+                send_final(j).start()
+
+        @pl.loop(0, CHUNKS)
+        def _(i):
+            send_across(i).wait_send()
+            send_outer(i).wait_send()
+
+    @pl.loop(0, CHUNKS)
+    def _(i):
+        share(i).wait_send()
+        send_final(i).wait()
+
+        @pl.loop(0, step_rows)
+        def _(r):
+            y = i * step_rows + r
+            total[(1 - core) * half_rows + y] = from_sib[y]
+
+
+def exchange_line(data, labels):
+    side, _, pieces, lanes = data.shape
+    half_rows = side // 2
+    me = lax.axis_index("patch")
+    z, core = me // 2, me % 2
+    near = z // 2
+    inner = (z == 1) | (z == 2)
+    everyone = lax.all_gather(labels, "patch", axis=0, tiled=False)
+    pair = jnp.stack([core, 1 - core])
+    chips = jnp.stack([3 * (1 - near), 2 - near, 3 * near, z])
+    order = (chips[:, None] * 2 + pair[None, :]).reshape(-1)
+    wanted = (order[:, None] * TILES + jnp.arange(TILES)[None, :]).reshape(-1)
+    mine = everyone[z * 2 + pair].reshape(-1)
+    theirs = everyone[3 * near * 2 + pair].reshape(-1)
+    of_mine = wanted[:, None] == mine[None, :]
+    to_outer = (jnp.arange(8 * TILES) // (2 * TILES)) == 2
+    of_theirs = (wanted[:, None] == theirs[None, :]) & ~to_outer[:, None]
+    inner_pick = jnp.concatenate([of_mine, of_theirs, of_mine, of_theirs], axis=1)
+    outer_pick = jnp.concatenate([of_mine, of_mine, of_mine, of_mine], axis=1)
+    pick = jnp.where(inner, inner_pick, outer_pick).astype(jnp.bfloat16)
+
+    def plane(count):
+        return pltpu.VMEM((half_rows, 2, count, lanes), jnp.float32)
+
+    many = pltpu.SemaphoreType.DMA((CHUNKS,))
+    return pl.pallas_call(
+        line_kernel,
+        out_shape=jax.ShapeDtypeStruct((side, 2, TILES, lanes), jnp.float32),
+        in_specs=[pl.BlockSpec(memory_space=pl.ANY), pl.BlockSpec(memory_space=pltpu.VMEM)],
+        out_specs=pl.BlockSpec(memory_space=pltpu.VMEM),
+        scratch_shapes=[
+            plane(2 * pieces), plane(2 * pieces), plane(4 * TILES), plane(4 * TILES),
+            plane(2 * TILES), plane(2 * TILES), plane(2 * TILES), plane(TILES), plane(TILES),
+            pltpu.SemaphoreType.DMA,
+        ] + [many] * 10,
+        compiler_params=pltpu.CompilerParams(
+            collective_id=0, has_side_effects=True, vmem_limit_bytes=48 * 1024 * 1024
+        ),
+        cost_estimate=pl.CostEstimate(flops=4 << 30, bytes_accessed=300 << 20, transcendentals=0),
+    )(data, pick)
+
+
+def coadd_kernel(total_ref, coadd_ref, term_ref):
+    side = total_ref.shape[1]
+    for ty in range(TILES_Y):
+        for tx in range(TILES_X):
+            tile = ty * TILES_X + tx
+            numer = total_ref[pl.ds(tile, side, stride=2 * TILES), :]
+            denom = total_ref[pl.ds(TILES + tile, side, stride=2 * TILES), :]
+            coadd = numer / jnp.maximum(denom, FLOOR)
+            spot = (slice(ty * side, (ty + 1) * side), slice(tx * side, (tx + 1) * side))
+            coadd_ref[spot] = coadd
+            term_ref[spot] = numer * coadd
+
+
+def per_device(images, coeffs, inverse_var, bad_lines, destinations, tile_slots):
+    owners_count = lax.axis_size("patch")
+    piece_count = images.shape[1]
+    if owners_count != 8 or piece_count != 32:
+        return exchanged_raw(images, coeffs, inverse_var, bad_lines, destinations, tile_slots)
+    tile_side = inverse_var.shape[-1]
+    half_taps = (images.shape[-1] - tile_side) // 2
+    bands = kernel_bands(tile_side, half_taps)
+    labels = destinations[0, :, 0] * TILES + tile_slots[0]
+    data = match_local(images[0], coeffs[0], inverse_var[0], bad_lines[0], bands)
+    total = exchange_line(data, labels)
+    shape = jax.ShapeDtypeStruct((TILES_Y * tile_side, TILES_X * tile_side), jnp.float32)
+    coadd, terms = pl.pallas_call(
+        coadd_kernel,
+        out_shape=(shape, shape),
+        compiler_params=pltpu.CompilerParams(vmem_limit_bytes=32 * 1024 * 1024),
+    )(total.reshape(-1, tile_side))
+    detection = lax.psum_scatter(terms, "band", scatter_dimension=0, tiled=True)
+    return (coadd[None, None], detection[None])
+
+
 def solution(mesh):
     in_specs = (
         P("band", "patch", None, None),

time: 725 us -> 241 us (0.33)
  waiting for transfers between devices: 526 us -> 29 us
  Pallas kernels: 0 us -> 166 us
  matrix products: 83.3 us -> 0 us
  local copies, waits for them, and re-layouts: 56.2 us -> 8.72 us
  starting transfers between devices: 32.6 us -> 0.04 us
  blocking collectives: 0 us -> 13.4 us
    all_to_all x4 -> x0, waiting for transfers between devices: 500 us -> none  [the longest x1 267 us: per_device(): lax.all_to_all(coeff_slots, 'patch', split_axis=0, concat_axis=0, tiled=T...]
    pallas_call x0 -> x3, Pallas kernels: none -> 166 us  [the longest x1 139 us: exchange_line(): pl.pallas_call(line_kernel, out_shape=jax.ShapeDtypeStruct((side, 2, TILE...]
    dot_general x7 -> x0, matrix products: 83.3 us -> none  [the longest x3 26.4 us: pack_slots(): jnp.dot(selector, flat_rows, precision=HIGHEST, preferred_element_type=jn...]
    all_to_all x4 -> x0, starting transfers between devices: 32.6 us -> none  [the longest x1 16.4 us: per_device(): lax.all_to_all(coeff_slots, 'patch', split_axis=0, concat_axis=0, tiled=T...]
    reshape x3 -> x0, local copies, waits for them, and re-layouts: 21.5 us -> none  [the longest x1 12.6 us: per_device(): coeff_part.reshape((-1,) + coeff_part.shape[2:])]
    all_to_all x3 -> x0, local copies, waits for them, and re-layouts: 19.2 us -> none  [the longest x1 11.2 us: per_device(): lax.all_to_all(coeff_slots, 'patch', split_axis=0, concat_axis=0, tiled=T...]
    all_gather x0 -> x1, blocking collectives: none -> 13.4 us  [exchange_line(): everyone = lax.all_gather(labels, 'patch', axis=0, tiled=False)]
  transfers between devices with their start and end apart: 5 -> 1, of which waited for: 4 -> 1; matrix products, arithmetic and copies ran while one was open for 19% -> 0% of each run, Pallas kernels for 0% -> 0%
where the time goes in v1:
time: 241 us; the launch traced here: 240 us
  Pallas kernels  166 us (69%)
  waiting for transfers between devices  29 us (12%)
  between operations  14.2 us (6%)
  blocking collectives  13.4 us (6%)
  other arithmetic  9.49 us (4%)
  local copies, waits for them, and re-layouts  8.72 us (4%)
    pallas_call x1, Pallas kernels, exchange_line(): pl.pallas_call(line_kernel, out_shape=jax.ShapeDtypeStruct((side, 2, TILE...  139 us
    reduce_scatter x1, waiting for transfers between devices, per_device(): detection = lax.psum_scatter(terms, 'band', scatter_dimension=0, tiled=True)  28.9 us
    pallas_call x1, Pallas kernels, match_local(): pl.pallas_call(match_kernel, out_shape=jax.ShapeDtypeStruct((side * 2 * c...  24.2 us
    all_gather x1, blocking collectives, exchange_line(): everyone = lax.all_gather(labels, 'patch', axis=0, tiled=False)  13.4 us
  transfers between devices with their start and end apart: 1, of which 1 were waited for; matrix products, arithmetic and copies ran while one was open for 0% of the time, Pallas kernels for 0%

profile of v1, /device:TPU:0, one launch (start us, length us, event | category | flops | bytes accessed | tf_op | source)
XLA Modules:
  0.0 240.4 jit_solution(1588079941103593559)
XLA Ops:
  7.2 0.0 copy-start.3
  7.2 0.0 copy-start.4
  7.2 0.0 copy-start.2
  7.2 0.0 reduce-scatter.2.cloned.1.call-start
  7.2 0.7 exponential_reduce_fusion.2
  7.9 0.6 exponential_reduce_fusion.1
  8.5 0.6 exponential_reduce_fusion
  9.2 0.6 compare_not_fusion
  9.7 0.7 divide_select_fusion.2
  10.4 1.4 divide_select_fusion
  11.8 0.0 copy-start
  11.8 0.7 fusion.6
  12.6 0.8 copy.19
  13.4 1.1 stack.42
  14.5 0.7 reduce_precision.16
  15.2 0.9 copy.21
  16.1 0.1 pad_add_fusion.4
  16.2 0.1 add_multiply_fusion.1
  16.3 0.1 add_multiply_fusion
  16.4 0.1 mul.97
  16.4 0.1 iota_add_fusion
  16.5 0.7 add.126
  17.2 0.0 copy-done.3
  17.2 0.0 copy-done.4
  17.2 13.4 %all-gather = s32[8,1,32]{2,1,0:T(1,128)S(1)} all-gather(s32[1,1,32]{2,1,0:T(1,128)S(1)} %fusion.13), channel_id=1, replica_groups=mesh['band'=4,'patch'=8] {'patch'}, dimensions={0}, use_global_device_ids=true | all-gather | bytes 1152 | tf_op jit(solution)/shard_map/all_gather | solution.py:368
  30.6 0.1 fusion.11
  30.7 0.6 gather_fusion
  31.2 0.6 eq.49
  31.8 0.6 gather_fusion.1
  32.4 0.6 eq.52
  33.0 0.0 copy-done.2
  33.0 0.1 copy.23.lines_ref
  33.1 1.1 copy.20
  34.2 1.0 pad_maximum_fusion.2.cols_ref
  35.2 1.1 fusion.14
  36.3 0.1 pad_maximum_fusion.rows_ref
  36.3 0.8 compare_and_fusion
  37.1 0.2 fusion.3.pick
  37.3 0.0 copy-done
  37.3 0.0 copy-start.1
  37.3 1.6 copy-done.1
  38.9 24.2 %shard_map.77 = f32[8192,128]{1,0:T(8,128)} custom-call(s32[32,2]{1,0:T(8,128)S(1)} %copy.23.lines_ref, f32[32,168,168]{2,1,0:T(8,128)} %bitcast.39, bf16[32,3,128,128]{3,2,1,0:T(8,128)(2,1)S(1)} %bitcast.34, f32[32,128,128]{2,1,0:T(8,128)S(1)} %bitcast.35, bf16[2,384,168]{2,1,0:T(8,128)(2,1)S(1)} %pad_maximum_fusion.rows_ref, ...), custom_call_target="tpu_custom_call" | custom-call | flops 9512681472 | bytes 14680064 | tf_op jit(solution)/shard_map/pallas_call | solution.py:159
  63.1 139.0 %shard_map.78 = f32[128,2,16,128]{3,2,1,0:T(8,128)S(1)} custom-call(f32[128,2,32,128]{3,2,1,0:T(8,128)} %bitcast.42, bf16[128,256]{1,0:T(8,128)(2,1)S(1)} %fusion.3.pick), custom_call_target="tpu_custom_call" | custom-call | flops 4294967296 | bytes 314572800 | tf_op jit(solution)/shard_map/pallas_call | solution.py:386
  202.1 2.6 %shard_map.79 = (f32[256,1024]{1,0:T(8,128)}, f32[256,1024]{1,0:T(8,128)}) custom-call(f32[4096,128]{1,0:T(8,128)S(1)} %bitcast.33), custom_call_target="tpu_custom_call" | custom-call | tf_op jit(solution)/shard_map/pallas_call | solution.py:428
  204.6 0.0 reduce-scatter.2.cloned.1.call-update
  204.6 28.9 %reduce-scatter.2.cloned.1.call-done = f32[64,1024]{1,0:T(8,128)} async-done(((f32[256,1024]{1,0:T(8,128)}), f32[64,1024]{1,0:T(8,128)}) %reduce-scatter.2.cloned.1.call-update) | async-done | bytes 262160 | tf_op jit(solution)/shard_map/reduce_scatter | solution.py:433
  (3 shorter events, 0.0 us)
Async XLA Ops:
  7.2 10.0 %copy-start.3 = (s32[1,32]{1,0:T(1,128)S(1)}, s32[1,32]{1,0:T(1,128)}, u32[]{:S(2)}) copy-start(s32[1,32]{1,0:T(1,128)} %param.11) | copy-start | bytes 388
  7.2 10.0 %copy-start.4 = (s32[1,32,1]{1,2,0:T(1,128)S(1)}, s32[1,32,1]{1,2,0:T(1,128)}, u32[]{:S(2)}) copy-start(s32[1,32,1]{1,2,0:T(1,128)} %param.10) | copy-start | bytes 388
  7.2 25.8 %copy-start.2 = (s32[1,32,2]{1,2,0:T(2,128)S(1)}, s32[1,32,2]{1,2,0:T(2,128)}, u32[]{:S(2)}) copy-start(s32[1,32,2]{1,2,0:T(2,128)} %param.9) | copy-start | bytes 772
  7.2 226.4 %reduce-scatter.2.cloned.1.call-start = ((), (), s32[]{:S(2)}) async-start(), calls=%async_computation.1 | async-start | bytes 1310720 | tf_op jit(solution)/shard_map/reduce_scatter | solution.py:433
  11.8 25.5 %copy-start = (bf16[1,32,3,128,128]{4,3,2,1,0:T(8,128)(2,1)S(1)}, bf16[1,32,3,128,128]{4,3,2,1,0:T(8,128)(2,1)}, u32[]{:S(2)}) copy-start(bf16[1,32,3,128,128]{4,3,2,1,0:T(8,128)(2,1)} %param.7) | copy-start | bytes 9437188
  37.3 1.6 copy-start.1
Sparse Core Ops, SparseCore 0:
  204.7 28.7 reduce-scatter.1

commit v2 on v1

--- a/solution.py
+++ b/solution.py
@@ -1,5 +1,6 @@
 import jax
 import jax.numpy as jnp
+import numpy as np
 from jax import lax
 from jax.experimental import pallas as pl
 from jax.experimental.pallas import tpu as pltpu
@@ -112,7 +113,7 @@
 
 TILES = TILES_Y * TILES_X
 GROUP = 4
-CHUNKS = 8
+CHUNKS = 16
 MESH = pl.DeviceIdType.MESH
 
 
@@ -149,13 +150,25 @@
         out_ref[pl.ds(count + piece, side, stride=2 * count), :] = weight
 
 
+def fixed_bands(tile_side, half_taps):
+    offset = np.arange(tile_side + 2 * half_taps)[None, :] - np.arange(tile_side)[:, None]
+    inside = (offset >= 0) & (offset <= 2 * half_taps)
+    taps = np.arange(2 * half_taps + 1) - half_taps
+    matrices = []
+    for fraction in FRACTIONS:
+        sigma = fraction * half_taps
+        total = np.sum(np.exp(-0.5 * (taps / sigma) ** 2))
+        matrices.append(np.where(inside, np.exp(-0.5 * ((offset - half_taps) / sigma) ** 2) / total, 0.0))
+    return np.stack(matrices).astype(np.float32)
+
+
 def match_local(images, coeffs, inverse_var, lines, bands):
     count, wide, _ = images.shape
     kernels, side, _ = bands.shape
-    rounded = lax.reduce_precision(bands, 8, 7)
-    high, low = rounded.astype(jnp.bfloat16), (bands - rounded).astype(jnp.bfloat16)
-    rows = jnp.stack([high.reshape(kernels * side, wide), low.reshape(kernels * side, wide)])
-    cols = jnp.concatenate([jnp.swapaxes(high, 1, 2), jnp.swapaxes(low, 1, 2)], axis=2)
+    high = bands.astype(jnp.bfloat16)
+    low = (bands - high.astype(np.float32)).astype(jnp.bfloat16)
+    rows = jnp.asarray(np.stack([high.reshape(kernels * side, wide), low.reshape(kernels * side, wide)]))
+    cols = jnp.asarray(np.concatenate([np.swapaxes(high, 1, 2), np.swapaxes(low, 1, 2)], axis=2))
     out = pl.pallas_call(
         match_kernel,
         out_shape=jax.ShapeDtypeStruct((side * 2 * count, side), jnp.float32),
@@ -365,13 +378,16 @@
     z, core = me // 2, me % 2
     near = z // 2
     inner = (z == 1) | (z == 2)
-    everyone = lax.all_gather(labels, "patch", axis=0, tiled=False)
+    others = [
+        lax.ppermute(labels, "patch", [(p, p ^ turn) for p in range(lax.axis_size("patch"))])
+        for turn in (1, 2, 3)
+    ]
     pair = jnp.stack([core, 1 - core])
     chips = jnp.stack([3 * (1 - near), 2 - near, 3 * near, z])
     order = (chips[:, None] * 2 + pair[None, :]).reshape(-1)
     wanted = (order[:, None] * TILES + jnp.arange(TILES)[None, :]).reshape(-1)
-    mine = everyone[z * 2 + pair].reshape(-1)
-    theirs = everyone[3 * near * 2 + pair].reshape(-1)
+    mine = jnp.concatenate([labels, others[0]])
+    theirs = jnp.concatenate([others[1], others[2]])
     of_mine = wanted[:, None] == mine[None, :]
     to_outer = (jnp.arange(8 * TILES) // (2 * TILES)) == 2
     of_theirs = (wanted[:, None] == theirs[None, :]) & ~to_outer[:, None]
@@ -416,11 +432,11 @@
 def per_device(images, coeffs, inverse_var, bad_lines, destinations, tile_slots):
     owners_count = lax.axis_size("patch")
     piece_count = images.shape[1]
-    if owners_count != 8 or piece_count != 32:
+    if owners_count != 8 or piece_count != 32 or lax.axis_size("band") != 4:
         return exchanged_raw(images, coeffs, inverse_var, bad_lines, destinations, tile_slots)
     tile_side = inverse_var.shape[-1]
     half_taps = (images.shape[-1] - tile_side) // 2
-    bands = kernel_bands(tile_side, half_taps)
+    bands = fixed_bands(tile_side, half_taps)
     labels = destinations[0, :, 0] * TILES + tile_slots[0]
     data = match_local(images[0], coeffs[0], inverse_var[0], bad_lines[0], bands)
     total = exchange_line(data, labels)
@@ -430,7 +446,17 @@
         out_shape=(shape, shape),
         compiler_params=pltpu.CompilerParams(vmem_limit_bytes=32 * 1024 * 1024),
     )(total.reshape(-1, tile_side))
-    detection = lax.psum_scatter(terms, "band", scatter_dimension=0, tiled=True)
+    band = lax.axis_index("band")
+    share = terms.shape[0] // 4
+
+    def block(index):
+        return lax.dynamic_slice_in_dim(terms, index * share, share, axis=0)
+
+    arrived = [
+        lax.ppermute(block(band ^ turn), "band", [(b, b ^ turn) for b in range(4)])
+        for turn in (3, 1, 2)
+    ]
+    detection = block(band) + arrived[1] + arrived[2] + arrived[0]
     return (coadd[None, None], detection[None])
 
 

time: 241 us -> 235 us (0.975)
  Pallas kernels: 166 us -> 206 us
  waiting for transfers between devices: 29 us -> 11.9 us
  between operations: 14.2 us -> 0.67 us
  blocking collectives: 13.4 us -> 0 us
  other arithmetic: 9.49 us -> 2.18 us
  starting transfers between devices: 0.04 us -> 6.73 us
    pallas_call x1, Pallas kernels: 139 us -> 180 us  [exchange_line(): pl.pallas_call(line_kernel, out_shape=jax.ShapeDtypeStruct((side, 2, TILE...]
    reduce_scatter x1 -> x0, waiting for transfers between devices: 28.9 us -> none  [per_device(): detection = lax.psum_scatter(terms, 'band', scatter_dimension=0, tiled=True)]
    all_gather x1 -> x0, blocking collectives: 13.4 us -> none  [exchange_line(): everyone = lax.all_gather(labels, 'patch', axis=0, tiled=False)]
    ppermute x0 -> x6, waiting for transfers between devices: none -> 11.9 us  [the longest x3 11.9 us: per_device(): lax.ppermute(block(band ^ turn), 'band', [(b, b ^ turn) for b in range(4)])]
    ppermute x0 -> x6, starting transfers between devices: none -> 6.73 us  [the longest x3 3.55 us: per_device(): lax.ppermute(block(band ^ turn), 'band', [(b, b ^ turn) for b in range(4)])]
    unnamed x10 -> x8, local copies, waits for them, and re-layouts: 1.61 us -> 5.42 us
    another operation x3 -> x0, local copies, waits for them, and re-layouts: 2.85 us -> none  [kernel_bands(): return jnp.stack(matrices)]
  transfers between devices with their start and end apart: 1 -> 6, of which waited for: 1 -> 2; matrix products, arithmetic and copies ran while one was open for 0% -> 1% of each run, Pallas kernels for 0% -> 10%
where the time goes in v2:
time: 235 us; the launch traced here: 234 us
  Pallas kernels  206 us (88%)
  waiting for transfers between devices  11.9 us (5%)
  starting transfers between devices  6.73 us (3%)
  local copies, waits for them, and re-layouts  6.42 us (3%)
    pallas_call x1, Pallas kernels, exchange_line(): pl.pallas_call(line_kernel, out_shape=jax.ShapeDtypeStruct((side, 2, TILE...  180 us
    pallas_call x1, Pallas kernels, match_local(): pl.pallas_call(match_kernel, out_shape=jax.ShapeDtypeStruct((side * 2 * c...  24.1 us
    ppermute x3, waiting for transfers between devices, per_device(): lax.ppermute(block(band ^ turn), 'band', [(b, b ^ turn) for b in range(4)])  11.9 us
    unnamed x8, local copies, waits for them, and re-layouts  5.42 us
  transfers between devices with their start and end apart: 6, of which 2 were waited for; matrix products, arithmetic and copies ran while one was open for 1% of the time, Pallas kernels for 10%

profile of v2, /device:TPU:0, one launch (start us, length us, event | category | flops | bytes accessed | tf_op | source)
XLA Modules:
  0.0 234.2 jit_solution(9031028209953353778)
XLA Ops:
  0.6 0.7 bitcast_add_fusion
  1.3 3.0 %collective-permute-start.1 = (s32[32]{0:T(128)S(1)}, s32[32]{0:T(128)S(1)}, u32[]{:S(2)}, u32[]{:S(2)}) collective-permute-start(s32[32]{0:T(128)S(1)} %bitcast_add_fusion), channel_id=1, source_target_pairs={{0,2},{1,3},{2,0},{3,1},{4,6},{5,7},{6,4},{7,5},{8,10},{9,11},{10,... | collective-permute-start | bytes 392 | tf_op jit(solution)/shard_map/ppermute | solution.py:382
  4.3 0.0 collective-permute-start.2
  4.3 0.1 collective-permute-start
  4.5 0.1 pad_add_fusion.4
  4.6 0.1 add_multiply_fusion.1
  4.6 0.1 add_multiply_fusion
  4.7 0.1 mul.50
  4.8 0.1 iota_add_fusion
  4.9 0.1 add.81
  5.0 0.8 copy.11.lines_ref
  5.7 0.0 copy-start
  5.7 1.9 copy-done
  7.6 0.0 copy-start.1
  7.6 1.6 copy-done.1
  9.2 0.0 copy-start.2
  9.2 1.0 copy-done.2
  10.2 0.0 copy-start.3
  10.2 0.9 copy-done.3
  11.2 24.1 %shard_map.95 = f32[8192,128]{1,0:T(8,128)} custom-call(s32[32,2]{1,0:T(8,128)S(1)} %copy.11.lines_ref, f32[32,168,168]{2,1,0:T(8,128)} %bitcast.23, bf16[32,3,128,128]{3,2,1,0:T(8,128)(2,1)S(1)} %bitcast.20, f32[32,128,128]{2,1,0:T(8,128)S(1)} %bitcast.21, bf16[2,384,168]{2,1,0:T(8,128)(2,1)S(1)} %copy-done.2, bf16[3,168,256]{2,1,0:T(8,128)(2,1)S(1)} %copy-done.3), custom_call_target="tpu_custom_call" | custom-call | flops 9512681472 | bytes 14680064 | tf_op jit(solution)/shard_map/pallas_call | solution.py:172
  35.2 0.0 collective-permute-done
  35.2 0.1 pad_add_fusion.5
  35.3 0.0 collective-permute-done.1
  35.3 0.0 collective-permute-done.2
  35.3 0.1 pad_add_fusion.6
  35.4 0.1 compare_and_fusion
  35.5 0.2 fusion.2.pick
  35.7 180.0 %shard_map.96 = f32[128,2,16,128]{3,2,1,0:T(8,128)S(1)} custom-call(f32[128,2,32,128]{3,2,1,0:T(8,128)} %bitcast.25, bf16[128,256]{1,0:T(8,128)(2,1)S(1)} %fusion.2.pick), custom_call_target="tpu_custom_call" | custom-call | flops 4294967296 | bytes 314572800 | tf_op jit(solution)/shard_map/pallas_call | solution.py:402
  215.7 2.3 shard_map.97
  217.9 0.1 constant_dynamic-slice_fusion.2
  218.0 1.5 collective-permute-start.3
  219.5 1.5 collective-permute-start.4
  221.1 0.5 collective-permute-start.5
  221.6 5.6 %collective-permute-done.3 = f32[64,1024]{1,0:T(8,128)S(1)} collective-permute-done((f32[64,1024]{1,0:T(8,128)S(1)}, f32[64,1024]{1,0:T(8,128)S(1)}, u32[]{:S(2)}, u32[]{:S(2)}) %collective-permute-start.3) | collective-permute-done | bytes 262176 | tf_op jit(solution)/shard_map/ppermute | solution.py:456
  227.2 6.2 %collective-permute-done.4 = f32[64,1024]{1,0:T(8,128)S(1)} collective-permute-done((f32[64,1024]{1,0:T(8,128)S(1)}, f32[64,1024]{1,0:T(8,128)S(1)}, u32[]{:S(2)}, u32[]{:S(2)}) %collective-permute-start.4) | collective-permute-done | bytes 262176 | tf_op jit(solution)/shard_map/ppermute | solution.py:456
  233.4 0.0 collective-permute-done.5
  233.4 0.8 add_bitcast_fusion
  (1 shorter events, 0.0 us)
Async XLA Ops:
  1.3 34.0 %collective-permute-start.1 = (s32[32]{0:T(128)S(1)}, s32[32]{0:T(128)S(1)}, u32[]{:S(2)}, u32[]{:S(2)}) collective-permute-start(s32[32]{0:T(128)S(1)} %bitcast_add_fusion), channel_id=1, source_target_pairs={{0,2},{1,3},{2,0},{3,1},{4,6},{5,7},{6,4},{7,5},{8,10},{9,11},{10,... | collective-permute-start | bytes 392 | tf_op jit(solution)/shard_map/ppermute | solution.py:382
  4.3 31.0 %collective-permute-start.2 = (s32[32]{0:T(128)S(1)}, s32[32]{0:T(128)S(1)}, u32[]{:S(2)}, u32[]{:S(2)}) collective-permute-start(s32[32]{0:T(128)S(1)} %bitcast_add_fusion), channel_id=1, source_target_pairs={{0,3},{1,2},{2,1},{3,0},{4,7},{5,6},{6,5},{7,4},{8,11},{9,10},{10,... | collective-permute-start | bytes 392 | tf_op jit(solution)/shard_map/ppermute | solution.py:382
  4.3 30.9 %collective-permute-start = (s32[32]{0:T(128)S(1)}, s32[32]{0:T(128)S(1)}, u32[]{:S(2)}, u32[]{:S(2)}) collective-permute-start(s32[32]{0:T(128)S(1)} %bitcast_add_fusion), channel_id=1, source_target_pairs={{0,1},{1,0},{2,3},{3,2},{4,5},{5,4},{6,7},{7,6},{8,9},{9,8},{10,11... | collective-permute-start | bytes 392 | tf_op jit(solution)/shard_map/ppermute | solution.py:382
  5.7 1.9 copy-start
  7.6 1.6 copy-start.1
  9.2 1.0 copy-start.2
  10.2 0.9 copy-start.3
  218.0 9.2 %collective-permute-start.3 = (f32[64,1024]{1,0:T(8,128)S(1)}, f32[64,1024]{1,0:T(8,128)S(1)}, u32[]{:S(2)}, u32[]{:S(2)}) collective-permute-start(f32[64,1024]{1,0:T(8,128)S(1)} %get-tuple-element.6), channel_id=1, source_target_pairs={{0,8},{8,0},{16,24},{24,16},{1,9},{9,1},{17,25},{25,17},{2,10},{10... | collective-permute-start | bytes 786440 | tf_op jit(solution)/shard_map/ppermute | solution.py:456
  219.5 13.9 %collective-permute-start.4 = (f32[64,1024]{1,0:T(8,128)S(1)}, f32[64,1024]{1,0:T(8,128)S(1)}, u32[]{:S(2)}, u32[]{:S(2)}) collective-permute-start(f32[64,1024]{1,0:T(8,128)S(1)} %get-tuple-element.8), channel_id=1, source_target_pairs={{0,16},{8,24},{16,0},{24,8},{1,17},{9,25},{17,1},{25,9},{2,18},{10... | collective-permute-start | bytes 786440 | tf_op jit(solution)/shard_map/ppermute | solution.py:456
  221.1 12.4 %collective-permute-start.5 = (f32[64,1024]{1,0:T(8,128)S(1)}, f32[64,1024]{1,0:T(8,128)S(1)}, u32[]{:S(2)}, u32[]{:S(2)}) collective-permute-start(f32[64,1024]{1,0:T(8,128)S(1)} %get-tuple-element.7), channel_id=1, source_target_pairs={{0,24},{8,16},{16,8},{24,0},{1,25},{9,17},{17,9},{25,1},{2,26},{10... | collective-permute-start | bytes 786440 | tf_op jit(solution)/shard_map/ppermute | solution.py:456
